TPU v7x, 512 devices: a whole 4x8x8 slice. The times are simulated.
512 devices in a mesh: ctx: 16 (over y, core), head: 4 (over x), seq: 8 (over z).
Axes of the slice: x: 4, y: 8, z: 8, core: 2. Of those that a mesh axis runs over, the one named last changes fastest.
Arguments:
- queries: bfloat16 [512, 128, 576], P('seq', 'head'), may hold values from -25 to 25
- latent_cache: bfloat16 [16384, 576], P('ctx'), may hold values from -12 to 12
- selected: int32 [512, 16, 384], P('seq', 'ctx'), may hold values from 0 to 1023, as said below
- counts: int32 [512, 16], P('seq', 'ctx'), may hold values from 1 to 384, 2048 in all within a row
- value_up: bfloat16 [4, 32, 512, 128], P('head', 'ctx'), may hold values from -0.25 to 0.25
- output_proj_weight: bfloat16 [4, 32, 128, 7168], P('head', 'ctx', None, 'seq'), may hold values from -0.046875 to 0.046875
Outputs:
- output: bfloat16 [512, 7168], P('seq', ('ctx', 'head'))
Inputs may be any that keep to these rules, and one draw needn't show every extreme that they name: In each row selected[q,s,:] all entries are distinct; the first counts[q,s] of them are the selected tokens, later entries are ignored. Each row of counts sums to 2048; its largest entry is exactly 384.
All inputs are finite; a program needn't handle non-finite values. No bound on the sum of `counts` on one device may be relied on, other than what follows from the above.
Results may differ from a plain program's by a relative error of at most 0.006.
Values may be sent and summed in bfloat16 or wider, within the bound.
A program may use at most 64 MiB of HBM per device.

v0:
```python
from functools import partial
import math

import jax
import jax.numpy as jnp
from jax import lax
from jax.sharding import PartitionSpec as P

LAT = 512
VDIM = 128


softmax_scale = (0.1 * math.log(40.0) + 1.0) ** 2 / math.sqrt(192.0)


def attend_group(packed, latent_cache):
    query_block_tile, rows_blk, count_blk = packed
    collected_latents = latent_cache[rows_blk]
    scores = (
        jnp.einsum(
            "epw,etw->ept", query_block_tile, collected_latents, preferred_element_type=jnp.float32
        )
        * softmax_scale
    )
    slot_ids = lax.broadcasted_iota(jnp.int32, scores.shape, 2)
    scores = jnp.where(slot_ids < count_blk[:, :, None], scores, -jnp.inf)
    peak_score = jnp.max(scores, axis=2, keepdims=True)
    weights = jnp.exp(scores - peak_score)
    totals = jnp.sum(weights, axis=2, keepdims=True)
    weighted = jnp.einsum(
        "bhk,bkl->bhl",
        weights.astype(jnp.bfloat16),
        collected_latents[:, :, :LAT],
        preferred_element_type=jnp.float32,
    )
    return (weighted / totals, (peak_score + jnp.log(totals))[:, :, 0])


def fold_sources(pieces):
    out_src, lse_src = pieces
    peak_score = jnp.max(lse_src, axis=0)
    factor = jnp.exp(lse_src - peak_score)
    norm_sum = jnp.sum(factor, axis=0)
    return jnp.sum(factor[..., None] * out_src, axis=0) / norm_sum[..., None]


def shards(queries, latent_cache, selected, counts, value_up, output_proj_weight):
    query_rows, number_of_heads, feature_width = queries.shape
    slot_count = selected.shape[2]
    group_size = max(
        (size_try for size_try in range(1, min(query_rows, 16) + 1) if query_rows % size_try == 0)
    )
    group_total = query_rows // group_size
    packed = (
        queries.reshape(group_total, group_size, number_of_heads, feature_width),
        selected.reshape(group_total, group_size, slot_count),
        counts.reshape(group_total, group_size, 1),
    )
    part_out, part_lse = lax.map(partial(attend_group, latent_cache=latent_cache), packed)
    part_out = part_out.reshape(query_rows, number_of_heads, LAT)
    part_lse = part_lse.reshape(query_rows, number_of_heads)
    head_share = number_of_heads // lax.axis_size("ctx")
    merged = fold_sources(
        (
            lax.all_to_all(part_out[None], "ctx", split_axis=2, concat_axis=0, tiled=True),
            lax.all_to_all(part_lse[None], "ctx", split_axis=2, concat_axis=0, tiled=True),
        )
    )
    merged = merged.astype(jnp.bfloat16)
    values = jnp.einsum(
        "qhl,hlv->qhv", merged, value_up[0], preferred_element_type=jnp.float32
    ).astype(jnp.bfloat16)
    flat = values.reshape(query_rows, head_share * VDIM)
    local_cols = output_proj_weight[0].reshape(head_share * VDIM, output_proj_weight.shape[3])
    terms = jnp.dot(
        flat,
        lax.all_gather(local_cols, "seq", axis=1, tiled=True),
        preferred_element_type=jnp.float32,
    )
    return lax.psum_scatter(terms, ("ctx", "head"), scatter_dimension=1, tiled=True).astype(
        jnp.bfloat16
    )


def solution(mesh):
    in_specs = (
        P("seq", "head", None),
        P("ctx", None),
        P("seq", "ctx", None),
        P("seq", "ctx"),
        P("head", "ctx", None, None),
        P("head", "ctx", None, "seq"),
    )
    out_specs = P("seq", ("ctx", "head"))
    return jax.shard_map(shards, mesh=mesh, in_specs=in_specs, out_specs=out_specs, check_vma=False)
```

profile of v0, /device:TPU:1, one launch (start us, length us, event | category | flops | bytes accessed | tf_op | source)
XLA Modules:
  0.0 438.3 jit_solution(3657880935607117874)
XLA Ops:
  7.1 1.4 reduce.4
  8.6 1.7 copy.43
  11.2 141.0 %while.12 = (s32[]{:T(128)}, f32[4,16,32,512]{3,1,0,2:T(8,128)}, f32[4,16,32]{2,1,0:T(8,128)S(1)}, s32[4,16,1]{1,2,0:T(1,128)S(1)}, bf16[4,16,32,576]{3,2,1,0:T(...) while((s32[]{:T(128)}, f32[4,16,32,512]{3,1,0,2:T(8,128)}, ...), condition=%wide.region_3.4_spmd, body=%wide.region_0.3_spmd.sunk | while | flops 429678080 | bytes 63003964 | solution.py:59
  11.2 25.9 %gather_fusion = bf16[6144,576]{1,0:T(8,128)(2,1)} fusion(bf16[1024,576]{1,0:T(8,128)(2,1)S(1)} %get-tuple-element.174, s32[6144]{0:T(1024)S(1)} %broadcast_clamp_fusion.2), kind=kCustom, calls=%fused_computation.clone.1 | custom fusion | bytes 14180352 | tf_op jit(solution)/shard_map/while/body/eval_jaxpr/gather | solution.py:18
  37.1 6.1 %fusion.35 = (f32[16,32]{1,0:T(8,128)S(1)}, f32[16,32,384]{2,1,0:T(8,128)S(1)}) fusion(bf16[16,384,576]{2,1,0:T(8,128)(2,1)} %bitcast.65, bf16[4,16,32,576]{3,2,1,0:T(8,128)(2,1)} %get-tuple-element.172, s32[]{:T(128)} %get-tuple-element.160, s32[16]{0:T(128)S(1)} %fusion.34), kind=kOutput, calls=%fused_computation.33.clone.1 | convolution fusion | flops 227278336 | bytes 9308736 | tf_op jit(solution)/shard_map/while/body/eval_jaxpr/epw,etw->ept/dot_general | solution.py:20
  44.8 1.6 copy_dynamic-update-slice_fusion.2
  46.4 25.9 %gather_fusion = bf16[6144,576]{1,0:T(8,128)(2,1)} fusion(bf16[1024,576]{1,0:T(8,128)(2,1)S(1)} %get-tuple-element.174, s32[6144]{0:T(1024)S(1)} %broadcast_clamp_fusion.2), kind=kCustom, calls=%fused_computation.clone.1 | custom fusion | bytes 14180352 | tf_op jit(solution)/shard_map/while/body/eval_jaxpr/gather | solution.py:18
  72.3 6.1 %fusion.35 = (f32[16,32]{1,0:T(8,128)S(1)}, f32[16,32,384]{2,1,0:T(8,128)S(1)}) fusion(bf16[16,384,576]{2,1,0:T(8,128)(2,1)} %bitcast.65, bf16[4,16,32,576]{3,2,1,0:T(8,128)(2,1)} %get-tuple-element.172, s32[]{:T(128)} %get-tuple-element.160, s32[16]{0:T(128)S(1)} %fusion.34), kind=kOutput, calls=%fused_computation.33.clone.1 | convolution fusion | flops 227278336 | bytes 9308736 | tf_op jit(solution)/shard_map/while/body/eval_jaxpr/epw,etw->ept/dot_general | solution.py:20
  78.8 1.3 divide_bitcast_fusion.2
  80.0 1.6 copy_dynamic-update-slice_fusion.2
  81.7 25.9 %gather_fusion = bf16[6144,576]{1,0:T(8,128)(2,1)} fusion(bf16[1024,576]{1,0:T(8,128)(2,1)S(1)} %get-tuple-element.174, s32[6144]{0:T(1024)S(1)} %broadcast_clamp_fusion.2), kind=kCustom, calls=%fused_computation.clone.1 | custom fusion | bytes 14180352 | tf_op jit(solution)/shard_map/while/body/eval_jaxpr/gather | solution.py:18
  107.6 6.1 %fusion.35 = (f32[16,32]{1,0:T(8,128)S(1)}, f32[16,32,384]{2,1,0:T(8,128)S(1)}) fusion(bf16[16,384,576]{2,1,0:T(8,128)(2,1)} %bitcast.65, bf16[4,16,32,576]{3,2,1,0:T(8,128)(2,1)} %get-tuple-element.172, s32[]{:T(128)} %get-tuple-element.160, s32[16]{0:T(128)S(1)} %fusion.34), kind=kOutput, calls=%fused_computation.33.clone.1 | convolution fusion | flops 227278336 | bytes 9308736 | tf_op jit(solution)/shard_map/while/body/eval_jaxpr/epw,etw->ept/dot_general | solution.py:20
  115.3 1.6 copy_dynamic-update-slice_fusion.2
  116.9 25.9 %gather_fusion = bf16[6144,576]{1,0:T(8,128)(2,1)} fusion(bf16[1024,576]{1,0:T(8,128)(2,1)S(1)} %get-tuple-element.174, s32[6144]{0:T(1024)S(1)} %broadcast_clamp_fusion.2), kind=kCustom, calls=%fused_computation.clone.1 | custom fusion | bytes 14180352 | tf_op jit(solution)/shard_map/while/body/eval_jaxpr/gather | solution.py:18
  142.8 6.1 %fusion.35 = (f32[16,32]{1,0:T(8,128)S(1)}, f32[16,32,384]{2,1,0:T(8,128)S(1)}) fusion(bf16[16,384,576]{2,1,0:T(8,128)(2,1)} %bitcast.65, bf16[4,16,32,576]{3,2,1,0:T(8,128)(2,1)} %get-tuple-element.172, s32[]{:T(128)} %get-tuple-element.160, s32[16]{0:T(128)S(1)} %fusion.34), kind=kOutput, calls=%fused_computation.33.clone.1 | convolution fusion | flops 227278336 | bytes 9308736 | tf_op jit(solution)/shard_map/while/body/eval_jaxpr/epw,etw->ept/dot_general | solution.py:20
  149.2 1.3 divide_bitcast_fusion.2
  150.5 1.7 copy_dynamic-update-slice_fusion.2
  153.5 16.3 %all_to_all.36 = f32[16,1,128]{2,1,0:T(1,128)S(1)} all-to-all(f32[16,1,128]{2,1,0:T(1,128)S(1)} %reshape.97), channel_id=1, replica_groups=mesh['ctx'=16,'head'=4,'seq'=8] {'ctx'}, dimensions={0} | all-to-all | bytes 16384 | tf_op jit(solution)/shard_map/all_to_all | solution.py:66
  169.8 4.9 %all-to-all-start.1 = ((f32[1,64,32,512]{3,1,0,2:T(8,128)}), f32[1,64,32,512]{3,1,0,2:T(8,128)}, u32[]{:S(2)}, u32[]{:S(2)}) async-start(f32[1,64,32,512]{3,1,0,2:T(8,128)} %bitcast.13), calls=%async_computation.1 | async-start | bytes 8388608 | tf_op jit(solution)/shard_map/all_to_all | solution.py:65
  176.7 91.8 %all-to-all-done.1 = f32[1,64,32,512]{3,1,0,2:T(8,128)} async-done(((f32[1,64,32,512]{3,1,0,2:T(8,128)}), f32[1,64,32,512]{3,1,0,2:T(8,128)}, u32[]{:S(2)}, u32[]{:S(2)}) %all-to-all-start.1) | async-done | bytes 4194336 | tf_op jit(solution)/shard_map/all_to_all | solution.py:65
  268.5 8.1 %fusion.13 = f32[64,2,512]{2,1,0:T(2,128)S(1)} fusion(f32[1,64,16,2,512]{4,1,3,2,0:T(8,128)} %bitcast.14, f32[16,64,2]{2,0,1:T(8,128)S(1)} %copy.45), kind=kLoop, calls=%fused_computation.22 | loop fusion | flops 2031616 | bytes 4464640 | tf_op jit(solution)/shard_map/reduce_sum | solution.py:44
  276.8 5.4 %convolution_bitcast_fusion = f32[7168,64]{1,0:T(8,128)} fusion(bf16[256,7168]{1,0:T(8,128)(2,1)} %all-gather.2.cloned.1.call-done, bf16[2,8,8,128]{3,2,1,0:T(8,128)(2,1)S(1)} %fusion.14), kind=kOutput, calls=%fused_computation.20 | convolution fusion | flops 234881024 | bytes 5537792
  282.2 147.7 %reduce-scatter.4.cloned.1.call-done = f32[112,64]{1,0:T(8,128)} async-done(((f32[7168,64]{1,0:T(8,128)}), f32[112,64]{1,0:T(8,128)}) %reduce-scatter.4.cloned.1.call-update) | async-done | bytes 28688
  429.9 1.5 copy.52
  (56 shorter events, 9.0 us)
Async XLA Ops:
  6.5 270.0 %copy-start = (bf16[1,2,512,128]{3,2,1,0:T(8,128)(2,1)S(1)}, bf16[1,2,512,128]{3,2,1,0:T(8,128)(2,1)}, u32[]{:S(2)}) copy-start(bf16[1,2,512,128]{3,2,1,0:T(8,128)(2,1)} %param.12) | copy-start | bytes 786436
  37.1 6.4 %copy-start.1 = (bf16[6144,576]{1,0:T(8,128)(2,1)S(1)}, bf16[6144,576]{1,0:T(8,128)(2,1)}, u32[]{:S(2)}) copy-start(bf16[6144,576]{1,0:T(8,128)(2,1)} %gather_fusion) | copy-start | bytes 21233668 | tf_op jit(solution)/shard_map/while
  72.3 6.4 %copy-start.1 = (bf16[6144,576]{1,0:T(8,128)(2,1)S(1)}, bf16[6144,576]{1,0:T(8,128)(2,1)}, u32[]{:S(2)}) copy-start(bf16[6144,576]{1,0:T(8,128)(2,1)} %gather_fusion) | copy-start | bytes 21233668 | tf_op jit(solution)/shard_map/while
  107.6 6.4 %copy-start.1 = (bf16[6144,576]{1,0:T(8,128)(2,1)S(1)}, bf16[6144,576]{1,0:T(8,128)(2,1)}, u32[]{:S(2)}) copy-start(bf16[6144,576]{1,0:T(8,128)(2,1)} %gather_fusion) | copy-start | bytes 21233668 | tf_op jit(solution)/shard_map/while
  142.8 6.4 %copy-start.1 = (bf16[6144,576]{1,0:T(8,128)(2,1)S(1)}, bf16[6144,576]{1,0:T(8,128)(2,1)}, u32[]{:S(2)}) copy-start(bf16[6144,576]{1,0:T(8,128)(2,1)} %gather_fusion) | copy-start | bytes 21233668 | tf_op jit(solution)/shard_map/while
  169.8 98.6 %all-to-all-start.1 = ((f32[1,64,32,512]{3,1,0,2:T(8,128)}), f32[1,64,32,512]{3,1,0,2:T(8,128)}, u32[]{:S(2)}, u32[]{:S(2)}) async-start(f32[1,64,32,512]{3,1,0,2:T(8,128)} %bitcast.13), calls=%async_computation.1 | async-start | bytes 8388608 | tf_op jit(solution)/shard_map/all_to_all | solution.py:65
  174.8 102.0 %all-gather.2.cloned.1.call-start = ((), (), s32[]{:S(2)}) async-start(), calls=%async_computation.3 | async-start | bytes 4128768 | tf_op jit(solution)/shard_map/all_gather | solution.py:77
  175.5 254.4 %reduce-scatter.4.cloned.1.call-start = ((), (), s32[]{:S(2)}) async-start(), calls=%async_computation.4 | async-start | bytes 3727360
Sparse Core Ops, SparseCore 0:
  177.7 56.5 all-gather.1
  282.4 147.4 reduce-scatter.3
where the time goes:
time: 443 us; the launch traced here: 438 us
  waiting for transfers between devices  240 us (54%)
  local copies, waits for them, and re-layouts  116 us (26%)
  matrix products  35.1 us (8%)
  blocking collectives  16.3 us (4%)
  between operations  13.5 us (3%)
  other arithmetic  12.2 us (3%)
  starting transfers between devices  5 us (1%)
    unnamed x3, waiting for transfers between devices  148 us
    gather x4, local copies, waits for them, and re-layouts, attend_group(): collected_latents = latent_cache[rows_blk]  104 us
    all_to_all x1, waiting for transfers between devices, shards(): lax.all_to_all(part_out[None], 'ctx', split_axis=2, concat_axis=0, tiled=...  91.8 us
    dot_general x4, matrix products, attend_group(): jnp.einsum('epw,etw->ept', query_block_tile, collected_latents, preferred...  24.4 us
    all_to_all x1, blocking collectives, shards(): lax.all_to_all(part_lse[None], 'ctx', split_axis=2, concat_axis=0, tiled=...  16.3 us
  transfers between devices with their start and end apart: 3, of which 2 were waited for; matrix products, arithmetic and copies ran while one was open for 2% of the time, Pallas kernels for 0%

commit v1 on v0

v1 whole, which is shorter than its diff:
```python
import functools
import math

import jax
import jax.numpy as jnp
from jax import lax
from jax.experimental import pallas as pl
from jax.experimental.pallas import tpu as pltpu
from jax.sharding import PartitionSpec as P

LAT = 512
VDIM = 128
LANES = 128
FAR = 1e30
MESH = pl.DeviceIdType.MESH
NY = 8
NZ = 8
NX = 4
Q = 64
BLOCK = 112
F32 = jnp.float32
BF16 = jnp.bfloat16

softmax_scale = (0.1 * math.log(40.0) + 1.0) ** 2 / math.sqrt(192.0)
exp2_scale = softmax_scale / math.log(2.0)


def dot_t(a, b):
    return lax.dot_general(a, b, (((1,), (1,)), ((), ())), preferred_element_type=F32)


def enter(peers):
    barrier = pltpu.get_barrier_semaphore()
    for peer in peers:
        pl.semaphore_signal(barrier, inc=1, device_id=peer, device_id_type=MESH)
    return barrier


def across(y, core):
    return lax.rem(y + NY, NY) * 2 + core


def attend_kernel(
    sel_ref, cnt_ref, q_ref, kv_ref, up_ref, out_ref,
    kv_buf, bias, q_own, s_buf, p_buf, part, lse, data_out, data_in, stat_out, stat_in,
    local_sem, pair_send, pair_recv, send_sem, recv_sem, stat_send, stat_recv,
):
    tokens, width = kv_ref.shape
    heads = q_ref.shape[1]
    slots = sel_ref.shape[1]
    tiles = tokens // LANES
    ctx = lax.axis_index("ctx")
    y, core = ctx // 2, lax.rem(ctx, 2)
    partner = {"ctx": y * 2 + 1 - core}
    sides = ({"ctx": across(y + 1, core)}, {"ctx": across(y - 1, core)})

    barrier = enter((partner,) + sides)
    own_kv = pltpu.make_async_copy(kv_ref, kv_buf.at[0], local_sem)
    own_kv.start()

    slot = lax.broadcasted_iota(jnp.int32, (1, slots), 1)
    tile_id = lax.broadcasted_iota(jnp.int32, (tiles, slots), 0)
    lane_id = lax.broadcasted_iota(jnp.int32, (LANES, slots), 0)

    pl.semaphore_wait(barrier, 3)
    pair_kv = pltpu.make_async_remote_copy(
        src_ref=kv_ref, dst_ref=kv_buf.at[1], send_sem=pair_send.at[0], recv_sem=pair_recv.at[0],
        device_id=partner, device_id_type=MESH,
    )
    pair_kv.start()

    def masks(g, carry):
        base = pl.multiple_of(g * 8, 8)
        sel = sel_ref[pl.ds(base, 8), :]
        cnt = cnt_ref[pl.ds(base, 8), :]
        fars = []
        for i in range(8):
            chosen = sel[i : i + 1, :]
            high = jnp.where(slot < cnt[i : i + 1, :], chosen >> 7, tiles)
            low = chosen & (LANES - 1)
            high_hot = (tile_id == high).astype(F32).astype(BF16)
            low_hot = (lane_id == low).astype(F32).astype(BF16)
            fars.append((dot_t(high_hot, low_hot) - 1.0) * FAR)
        for t in range(tiles):
            bias[0, pl.ds(base, 8), t * LANES : (t + 1) * LANES] = jnp.concatenate(
                [far[t : t + 1, :] for far in fars], axis=0
            )
        return carry

    lax.fori_loop(0, Q // 8, masks, 0)
    pair_bias = pltpu.make_async_remote_copy(
        src_ref=bias.at[0], dst_ref=bias.at[1], send_sem=pair_send.at[1], recv_sem=pair_recv.at[1],
        device_id=partner, device_id_type=MESH,
    )
    pair_bias.start()

    rows = lax.broadcasted_iota(jnp.int32, (256, 512), 0)
    cols = lax.broadcasted_iota(jnp.int32, (256, 512), 1)
    head = rows // 16
    wanted = (rows % 16) * heads + (head // 2) * 4 + core * 2 + head % 2
    pick = (cols == wanted).astype(F32).astype(BF16)
    for g in range(Q // 16):
        block = q_ref[g * 16 : (g + 1) * 16].reshape(512, width)
        own = jnp.dot(pick, block, preferred_element_type=F32).astype(BF16)
        q_own[:, g * 16 : (g + 1) * 16, :] = own.reshape(16, 16, width)

    own_kv.wait()
    pair_kv.wait()
    pair_bias.wait()

    def compute(unit, dests):
        for n, dest in enumerate(dests):
            q = q_own[pl.ds(dest * 2, 2)].reshape(128, width)
            for half in range(2):
                s_buf[n * 128 : (n + 1) * 128, half * tokens : (half + 1) * tokens] = dot_t(
                    q, kv_buf[half]
                )
        count = len(dests) * 128
        for r in range(0, count, 16):
            n, e, qs = r // 128, (r % 128) // 64, r % 64
            parts = []
            for half in range(2):
                for t in range(tiles):
                    a, b = half * tokens + t * LANES, t * LANES
                    parts.append(
                        s_buf[r : r + 16, a : a + LANES] + bias[half, qs : qs + 16, b : b + LANES]
                    )
            top = jnp.max(functools.reduce(jnp.maximum, parts), axis=1, keepdims=True)
            weights = [jnp.exp2((x - top) * exp2_scale) for x in parts]
            total = jnp.sum(functools.reduce(jnp.add, weights), axis=1, keepdims=True)
            for t, w in enumerate(weights):
                p_buf[r : r + 16, t * LANES : (t + 1) * LANES] = w.astype(BF16)
            value = top * softmax_scale + jnp.log(total)
            lse[n, e, qs : qs + 16, :] = jnp.broadcast_to(value, (16, LANES))
            part[n, e, qs : qs + 16, 0:LANES] = jnp.broadcast_to(1.0 / total, (16, LANES))
        for n in range(len(dests)):
            p = p_buf[n * 128 : (n + 1) * 128, :]
            o = jnp.dot(p[:, :tokens], kv_buf[0, :, :LAT], preferred_element_type=F32)
            o = o + jnp.dot(p[:, tokens:], kv_buf[1, :, :LAT], preferred_element_type=F32)
            for e in range(2):
                inv = part[n, e, :, 0:LANES]
                for t in range(LAT // LANES):
                    c = slice(t * LANES, (t + 1) * LANES)
                    part[n, e, :, c] = o[e * 64 : (e + 1) * 64, c] * inv

    def copies(side, u):
        return (
            pltpu.make_async_remote_copy(
                src_ref=data_out.at[side, u], dst_ref=data_in.at[side, u],
                send_sem=send_sem.at[side, u], recv_sem=recv_sem.at[side, u],
                device_id=sides[side], device_id_type=MESH,
            ),
            pltpu.make_async_remote_copy(
                src_ref=stat_out.at[side, u], dst_ref=stat_in.at[side, u],
                send_sem=stat_send.at[side, u], recv_sem=stat_recv.at[side, u],
                device_id=sides[side], device_id_type=MESH,
            ),
        )

    def send(side, u, values, level):
        for t in range(LAT // LANES):
            data_out[side, u, :, t * LANES : (t + 1) * LANES] = values[t].astype(BF16)
        stat_out[side, u] = jnp.concatenate([level, level], axis=0).T[0:8, :]
        for copy in copies(side, u):
            copy.start()

    def held(n, e):
        return [part[n, e, :, t * LANES : (t + 1) * LANES] for t in range(LAT // LANES)], lse[n, e]

    def merge(side, u, values, level):
        for copy in copies(side, u):
            copy.wait_recv()
        other = jnp.broadcast_to(stat_in[side, u, 0:1, :], (LANES, LANES)).T[0:64, :]
        top = jnp.maximum(other, level)
        w_in, w_own = jnp.exp(other - top), jnp.exp(level - top)
        total = w_in + w_own
        inv = 1.0 / total
        w_in, w_own = w_in * inv, w_own * inv
        mixed = [
            data_in[side, u, :, t * LANES : (t + 1) * LANES].astype(F32) * w_in + values[t] * w_own
            for t in range(LAT // LANES)
        ]
        return mixed, top + jnp.log(total)

    def dest(k):
        return lax.rem(y + k + NY, NY)

    compute(0, [dest(4)])
    for side in range(2):
        send(side, 0, *held(0, side))
    for hop in range(1, 4):
        compute(hop, [dest(4 - hop), dest(hop - 4)])
        base = 1 + 2 * (hop - 1)
        for order in range(2):
            for side in range(2):
                if hop == 1:
                    e = 1 - side if order == 0 else side
                    mine = held(side, e)
                    if order == 1:
                        mine = merge(side, 0, *mine)
                else:
                    e = 1 - side if order == 0 else side
                    mine = merge(side, base - 2 + e, *held(side, e))
                send(side, base + e, *mine)
    compute(4, [y])
    for e in range(2):
        mine = held(0, e)
        for side in range(2):
            mine = merge(side, 5 + e, *mine)
        merged = jnp.concatenate([m.astype(BF16) for m in mine[0]], axis=1)
        value = jnp.dot(merged, up_ref[e], preferred_element_type=F32)
        out_ref[:, e * VDIM : (e + 1) * VDIM] = value.astype(BF16)
    for side in range(2):
        for u in range(7):
            for copy in copies(side, u):
                copy.wait_send()


def attend(queries, latent_cache, selected, counts, value_up):
    rows, heads, width = queries.shape
    tokens = latent_cache.shape[0]
    vmem = pl.BlockSpec(memory_space=pltpu.VMEM)
    dma = pltpu.SemaphoreType.DMA
    return pl.pallas_call(
        attend_kernel,
        out_shape=jax.ShapeDtypeStruct((rows, 2 * VDIM), BF16),
        in_specs=[vmem, vmem, vmem, pl.BlockSpec(memory_space=pl.ANY), vmem],
        out_specs=vmem,
        scratch_shapes=[
            pltpu.VMEM((2, tokens, width), BF16),
            pltpu.VMEM((2, rows, tokens), F32),
            pltpu.VMEM((16, rows, width), BF16),
            pltpu.VMEM((256, 2 * tokens), F32),
            pltpu.VMEM((256, 2 * tokens), BF16),
            pltpu.VMEM((2, 2, rows, LAT), F32),
            pltpu.VMEM((2, 2, rows, LANES), F32),
            pltpu.VMEM((2, 7, rows, LAT), BF16),
            pltpu.VMEM((2, 7, rows, LAT), BF16),
            pltpu.VMEM((2, 7, 8, LANES), F32),
            pltpu.VMEM((2, 7, 8, LANES), F32),
            dma, dma((2,)), dma((2,)), dma((2, 7)), dma((2, 7)), dma((2, 7)), dma((2, 7)),
        ],
        compiler_params=pltpu.CompilerParams(
            collective_id=0, has_side_effects=True, vmem_limit_bytes=48 * 1024 * 1024
        ),
    )(selected, counts, queries, latent_cache, value_up)


def project_kernel(
    val_ref, w_ref, out_ref,
    vals, w_own, w_pair, own_x, x_out, x_in, z_out, z_in, y_in,
    w_send, w_recv, z_send, z_recv, c_send, c_recv, x_send, x_recv, a_send, a_recv, y_send, y_recv,
):
    ctx, x, z = lax.axis_index("ctx"), lax.axis_index("head"), lax.axis_index("seq")
    y, core = ctx // 2, lax.rem(ctx, 2)
    partner = {"ctx": y * 2 + 1 - core}

    def at_y(k):
        return {"ctx": across(y + k, core)}

    def at_x(k):
        return {"head": lax.rem(x + k + NX, NX)}

    def at_z(k):
        return {"seq": lax.rem(z + k + NZ, NZ)}

    barrier = enter(
        [partner]
        + [at_y(k) for k in range(1, NY)]
        + [at_x(k) for k in range(1, NX)]
        + [at_z(k) for k in range(1, NZ)]
    )
    rows = w_ref.shape[0]
    pad = jnp.zeros((rows, LANES - BLOCK), BF16)
    for k in range(NX):
        low = w_ref[:, k * BLOCK : (k + 1) * BLOCK]
        high = w_ref[:, (NX + k) * BLOCK : (NX + k + 1) * BLOCK]
        c = slice(k * LANES, (k + 1) * LANES)
        low = jnp.concatenate([low, pad], axis=1)
        high = jnp.concatenate([high, pad], axis=1)
        w_own[0, :, c] = jnp.where(core == 0, low, high)
        w_pair[:, c] = jnp.where(core == 0, high, low)
    vals[0, z] = val_ref[...]
    pl.semaphore_wait(barrier, 1 + (NY - 1) + (NX - 1) + (NZ - 1))

    def remote(src, dst, s, r, peer):
        return pltpu.make_async_remote_copy(
            src_ref=src, dst_ref=dst, send_sem=s, recv_sem=r, device_id=peer, device_id_type=MESH
        )

    order = [0, 1, 7, 2, 6, 3, 5, 4]
    gather = {
        d: remote(vals.at[0, z], vals.at[0, z], z_send.at[d], z_recv.at[d], at_z(d))
        for d in order[1:]
    }
    for d in order[1:]:
        gather[d].start()
    w_copy = remote(w_pair, w_own.at[1], w_send, w_recv, partner)
    w_copy.start()

    forward = {}
    for d in order:
        j = lax.rem(z - d + NZ, NZ)
        if d:
            arrival = remote(vals.at[0, j], vals.at[0, j], z_send.at[d], z_recv.at[d], at_z(d))
            arrival.wait_recv()
        forward[d] = remote(vals.at[0, j], vals.at[1, j], c_send.at[d], c_recv.at[d], partner)
        forward[d].start()
    w_copy.wait()

    cross = {}
    for d in order:
        j = lax.rem(z - d + NZ, NZ)
        forward[d].wait_recv()
        terms = jnp.dot(vals[0, j], w_own[0], preferred_element_type=F32)
        terms = terms + jnp.dot(vals[1, j], w_own[1], preferred_element_type=F32)
        for k in range(NX):
            x_out[d, k] = terms[:, k * LANES : (k + 1) * LANES]
        own_x[d] = x_out[d, x]
        for k in range(1, NX):
            peer = lax.rem(x + k, NX)
            z_out[d, k] = x_out[d, peer].astype(BF16)
            cross[d, k] = remote(
                z_out.at[d, k], x_in.at[d, k], x_send.at[d, k], x_recv.at[d, k], at_x(k)
            )
            cross[d, k].start()

    spread = {}
    for d in order:
        total = own_x[d]
        for k in range(1, NX):
            cross[d, k].wait_recv()
            total = total + x_in[d, k].astype(F32)
        if d == 0:
            z_in[z] = total.astype(BF16)
        else:
            z_out[d, 0] = total.astype(BF16)
            spread[d] = remote(z_out.at[d, 0], z_in.at[z], a_send.at[d], a_recv.at[d], at_z(-d))
            spread[d].start()
    for d in order[1:]:
        spread[d].wait_recv()

    last = {}
    for k in [1, 7, 2, 6, 3, 5, 4]:
        target = lax.rem(y + k, NY)
        last[k] = remote(z_in.at[target], y_in.at[k], y_send.at[k], y_recv.at[k], at_y(k))
        last[k].start()
    total = z_in[y].astype(F32)
    for k in [1, 7, 2, 6, 3, 5, 4]:
        last[k].wait_recv()
        total = total + y_in[k].astype(F32)
    out_ref[...] = total[:, :BLOCK].astype(BF16)
    for d in order:
        if d:
            gather[d].wait_send()
            spread[d].wait_send()
        forward[d].wait_send()
        for k in range(1, NX):
            cross[d, k].wait_send()
    for k in range(1, NY):
        last[k].wait_send()


def project(values, weight):
    rows = values.shape[0]
    vmem = pl.BlockSpec(memory_space=pltpu.VMEM)
    dma = pltpu.SemaphoreType.DMA
    return pl.pallas_call(
        project_kernel,
        out_shape=jax.ShapeDtypeStruct((rows, BLOCK), BF16),
        in_specs=[vmem, vmem],
        out_specs=vmem,
        scratch_shapes=[
            pltpu.VMEM((2, NZ, rows, 2 * VDIM), BF16),
            pltpu.VMEM((2, 2 * VDIM, NX * LANES), BF16),
            pltpu.VMEM((2 * VDIM, NX * LANES), BF16),
            pltpu.VMEM((NZ, rows, LANES), F32),
            pltpu.VMEM((NZ, NX, rows, LANES), F32),
            pltpu.VMEM((NZ, NX, rows, LANES), BF16),
            pltpu.VMEM((NZ, NX, rows, LANES), BF16),
            pltpu.VMEM((NZ, rows, LANES), BF16),
            pltpu.VMEM((NY, rows, LANES), BF16),
            dma, dma, dma((NZ,)), dma((NZ,)), dma((NZ,)), dma((NZ,)), dma((NZ, NX)), dma((NZ, NX)),
            dma((NZ,)), dma((NZ,)), dma((NY,)), dma((NY,)),
        ],
        compiler_params=pltpu.CompilerParams(
            collective_id=1, has_side_effects=True, vmem_limit_bytes=32 * 1024 * 1024
        ),
    )(values, weight)


def shards(queries, latent_cache, selected, counts, value_up, output_proj_weight):
    weight = output_proj_weight[0].reshape(2 * VDIM, output_proj_weight.shape[3])
    values = attend(queries, latent_cache, selected[:, 0, :], counts, value_up[0])
    return project(values, weight)


def solution(mesh):
    in_specs = (
        P("seq", "head", None),
        P("ctx", None),
        P("seq", "ctx", None),
        P("seq", "ctx"),
        P("head", "ctx", None, None),
        P("head", "ctx", None, "seq"),
    )
    out_specs = P("seq", ("ctx", "head"))
    return jax.shard_map(shards, mesh=mesh, in_specs=in_specs, out_specs=out_specs, check_vma=False)
```

time: 443 us -> 73.2 us (0.17)
  the two profiles are of different devices: /device:TPU:1 before, /device:TPU:8 now
where the time goes in v1:
time: 73.2 us; the launch traced here: 73 us
  Pallas kernels  67.2 us (92%)
  local copies, waits for them, and re-layouts  5.71 us (8%)
    pallas_call x1, Pallas kernels, project(): pl.pallas_call(project_kernel, out_shape=jax.ShapeDtypeStruct((rows, BLOC...  36.7 us
    pallas_call x1, Pallas kernels, attend(): pl.pallas_call(attend_kernel, out_shape=jax.ShapeDtypeStruct((rows, 2 * V...  30.5 us
    unnamed x10, local copies, waits for them, and re-layouts  5.71 us

profile of v1, /device:TPU:8, one launch (start us, length us, event | category | flops | bytes accessed | tf_op | source)
XLA Modules:
  0.0 73.0 jit_solution(2274417011075612888)
XLA Ops:
  0.0 0.7 %copy.7.cnt_ref = s32[64,1]{1,0:T(8,128)S(1)} copy(s32[64,1]{0,1:T(1,128)} %param.9) | data formatting | bytes 512 | tf_op args[3]
  0.7 0.0 copy-start.2
  0.7 0.9 %copy.11 = s32[64,1,384]{2,0,1:T(8,128)S(1)} copy(s32[64,1,384]{2,1,0:T(1,128)} %param.8) | data formatting | bytes 196608
  1.7 1.7 %copy.8.kv_ref = bf16[1024,576]{1,0:T(8,128)(2,1)S(1)} copy(bf16[1024,576]{0,1:T(8,128)(2,1)} %param.7) | data formatting | bytes 2359296 | tf_op args[1]
  3.4 0.0 copy-done.2
  3.4 0.0 copy-start
  3.4 1.7 %copy-done = bf16[64,32,576]{2,1,0:T(8,128)(2,1)S(1)} copy-done((bf16[64,32,576]{2,1,0:T(8,128)(2,1)S(1)}, bf16[64,32,576]{2,1,0:T(8,128)(2,1)}, u32[]{:S(2)}) %copy-start) | copy-done | bytes 2359320
  5.1 0.0 copy-start.1
  5.1 30.5 %shard_map.64.val_ref = bf16[64,256]{1,0:T(8,128)(2,1)S(1)} custom-call(s32[64,384]{1,0:T(8,128)S(1)} %bitcast.6, s32[64,1]{1,0:T(8,128)S(1)} %copy.7.cnt_ref, bf16[64,32,576]{2,1,0:T(8,128)(2,1)S(1)} %copy-done, bf16[1024,576]{1,0:T(8,128)(2,1)S(1)} %copy.8.kv_ref, bf16[2,512,128]{2,1,0:T(8,128)(2,1)S(1)} %bitcast.7), custom_call_target="tpu_custom_call" | custom-call | tf_op jit(solution)/shard_map/pallas_call | solution.py:224
  35.6 0.0 copy-done.1
  35.6 36.7 %shard_map.65 = bf16[64,112]{1,0:T(8,128)(2,1)S(1)} custom-call(bf16[64,256]{1,0:T(8,128)(2,1)S(1)} %shard_map.64.val_ref, bf16[256,896]{1,0:T(8,128)(2,1)S(1)} %bitcast.5), custom_call_target="tpu_custom_call" | custom-call | tf_op jit(solution)/shard_map/pallas_call | solution.py:368
  72.4 0.6 copy.13
Async XLA Ops:
  0.7 2.6 %copy-start.2 = (bf16[1,2,512,128]{3,2,1,0:T(8,128)(2,1)S(1)}, bf16[1,2,512,128]{3,2,1,0:T(8,128)(2,1)}, u32[]{:S(2)}) copy-start(bf16[1,2,512,128]{3,2,1,0:T(8,128)(2,1)} %param.10) | copy-start | bytes 786436
  3.4 1.7 %copy-start = (bf16[64,32,576]{2,1,0:T(8,128)(2,1)S(1)}, bf16[64,32,576]{2,1,0:T(8,128)(2,1)}, u32[]{:S(2)}) copy-start(bf16[64,32,576]{2,1,0:T(8,128)(2,1)} %q_ref.1) | copy-start | bytes 7077892
  5.1 30.5 %copy-start.1 = (bf16[1,2,128,896]{3,2,1,0:T(8,128)(2,1)S(1)}, bf16[1,2,128,896]{3,2,1,0:T(8,128)(2,1)}, u32[]{:S(2)}) copy-start(bf16[1,2,128,896]{3,2,1,0:T(8,128)(2,1)} %param.11) | copy-start | bytes 1376260

commit v2 on v0

v2 whole, which is shorter than its diff:
```python
import functools
import math

import jax
import jax.numpy as jnp
from jax import lax
from jax.experimental import pallas as pl
from jax.experimental.pallas import tpu as pltpu
from jax.sharding import PartitionSpec as P

LAT = 512
VDIM = 128
LANES = 128
FAR = 1e30
MESH = pl.DeviceIdType.MESH
NY = 8
NZ = 8
NX = 4
Q = 64
BLOCK = 112
F32 = jnp.float32
BF16 = jnp.bfloat16

softmax_scale = (0.1 * math.log(40.0) + 1.0) ** 2 / math.sqrt(192.0)
exp2_scale = softmax_scale / math.log(2.0)


def iota(shape, axis):
    return lax.broadcasted_iota(jnp.int32, shape, axis)


def dot(a, b):
    return jnp.dot(a, b, preferred_element_type=F32)


def remote(src, dst, s, r, peer):
    return pltpu.make_async_remote_copy(
        src_ref=src, dst_ref=dst, send_sem=s, recv_sem=r, device_id=peer, device_id_type=MESH
    )


def lane_tiles(width):
    return [slice(t * LANES, (t + 1) * LANES) for t in range(width // LANES)]


def build_bias(sel_v, cnt_v, words, bias):
    tokens = bias.shape[1]
    lane = iota((1, LANES), 1)
    s = sel_v[...].reshape(Q, 384).astype(F32)
    first = jnp.concatenate([s[:, 0:128], s[:, 128:256]], axis=0).T
    last = jnp.concatenate([s[:, 256:384], s[:, 256:384]], axis=0).T
    last = jnp.where(lane < 64, last[0:64], last[64:128])
    sel_t = jnp.concatenate([first, last], axis=0).astype(jnp.int32)
    row = iota((192, LANES), 0)
    late = (iota((192, LANES), 1) >= 64).astype(jnp.int32)
    slot = jnp.where(row < 128, row + 128 * late, row + 128 + 64 * late)
    cnt = cnt_v[...]
    cnt = jnp.concatenate([cnt, cnt], axis=1)
    high = sel_t >> 4
    value = jnp.where(slot < cnt, (1 << (sel_t & 15)).astype(F32), 0.0)
    for k in range(64):
        words[k : k + 1, :] = jnp.sum(jnp.where(high == k, value, 0.0), axis=0, keepdims=True)
    w = words[...]
    w = (w + pltpu.roll(w, 64, 1)).astype(jnp.int32)
    bytes_t = jnp.concatenate([(w & 255).astype(F32), (w >> 8).astype(F32)], axis=0).T
    token = iota((128, tokens), 1)
    place = ((token >> 3) & 1) * 64 + (token >> 4)
    expand = (place == iota((128, tokens), 0)).astype(F32).astype(BF16)
    found = dot(bytes_t[0:Q].astype(BF16), expand).astype(jnp.int32)
    bit = (found >> (iota((Q, tokens), 1) & 7)) & 1
    bias[...] = jnp.where(bit == 1, 0.0, -FAR)


def kernel(
    sel_ref, cnt_ref, q_ref, kvt_ref, up_ref, w_ref, out_ref,
    sel_v, cnt_v, q_v, kvt_v, up_v, w_v, local_sem,
    words, bias, kv_v, q_t, s_buf, p_buf, inv_buf,
    part, lse, pair_in, pair_lse, pair_send, pair_recv, own, own_lse,
    data_out, data_in, stat_out, stat_in, ring_send, ring_recv,
    val_v, vals, w_all, w_send, w_recv, twin_send, twin_recv, z_send, z_recv,
    x_f, x_out, x_in, x_send, x_recv, z_out, z_in, a_send, a_recv, y_in, y_send, y_recv,
):
    width = kvt_ref.shape[0]
    ctx, x, z = lax.axis_index("ctx"), lax.axis_index("head"), lax.axis_index("seq")
    y, core = ctx // 2, lax.rem(ctx, 2)
    partner = {"ctx": y * 2 + 1 - core}

    def at_y(k):
        return {"ctx": lax.rem(y + k + NY, NY) * 2 + core}

    def at_z(k, c):
        return {"ctx": y * 2 + c, "seq": lax.rem(z + k + NZ, NZ)}

    def at_x(k):
        return {"head": lax.rem(x + k, NX)}

    def fetch(i, src, dst):
        copy = pltpu.make_async_copy(src, dst, local_sem.at[i])
        copy.start()
        return copy

    fetch_sel = fetch(0, sel_ref, sel_v)
    fetch_cnt = fetch(1, cnt_ref, cnt_v)
    fetch_kvt = fetch(2, kvt_ref, kvt_v)
    first_half = lax.rem(y + 4, NY) // 4
    halves = (first_half, 1 - first_half)
    fetch_q = [
        fetch(3 + i, q_ref.at[:, pl.ds(pl.multiple_of(half * 16, 16), 16), :], q_v.at[i])
        for i, half in enumerate(halves)
    ]
    fetch_up = fetch(5, up_ref, up_v)
    fetch_w = fetch(6, w_ref, w_v.at[0])

    barrier = pltpu.get_barrier_semaphore()
    peers = [partner] + [at_y(k) for k in range(1, NY)] + [at_x(k) for k in range(1, NX)]
    peers += [at_z(k, c) for k in range(1, NZ) for c in range(2)]
    for peer in peers:
        pl.semaphore_signal(barrier, inc=1, device_id=peer, device_id_type=MESH)

    fetch_sel.wait()
    fetch_cnt.wait()
    build_bias(sel_v, cnt_v, words, bias)
    fetch_kvt.wait()
    kv_v[...] = kvt_v[0:LAT, :].T
    r, c = iota((256, 256), 0), iota((256, 256), 1)
    swap = (c == (r & 15) * 16 + (r >> 4)).astype(F32).astype(BF16)

    def by_head(i):
        fetch_q[i].wait()
        for g in range(Q // 16):
            block = q_v[i, g * 16 : (g + 1) * 16].reshape(256, width)
            q_t[pl.ds(halves[i] * 16, 16), g * 16 : (g + 1) * 16, :] = (
                dot(swap, block).astype(BF16).reshape(16, 16, width)
            )

    by_head(0)

    def dest(u, n):
        return lax.rem(y + (4 - u if n == 0 else u - 4) + NY, NY)

    sequence = ((0, 0), (1, 0), (1, 1), (2, 0), (2, 1), (3, 0), (3, 1), (4, 0))

    def score(i):
        q = q_t[pl.ds(dest(*sequence[i]) * 4, 4)].reshape(256, width)
        s_buf[i % 2] = dot(q, kvt_v[...])

    def compute(i):
        if 0 < i < len(sequence) - 1:
            score(i + 1)
        (u, n), m = sequence[i], i % 2
        for r in range(0, 256, 16):
            h, qs = r // 64, r % 64
            parts = [s_buf[m, r : r + 16, t] + bias[qs : qs + 16, t] for t in lane_tiles(1024)]
            top = jnp.max(functools.reduce(jnp.maximum, parts), axis=1, keepdims=True)
            weights = [jnp.exp2((part - top) * exp2_scale) for part in parts]
            total = jnp.sum(functools.reduce(jnp.add, weights), axis=1, keepdims=True)
            for t, value in zip(lane_tiles(1024), weights):
                p_buf[m, r : r + 16, t] = value.astype(BF16)
            level = top * softmax_scale + jnp.log(total)
            lse[u, n, h, qs : qs + 16, :] = jnp.broadcast_to(level, (16, LANES))
            inv_buf[m, r : r + 16, :] = jnp.broadcast_to(1.0 / total, (16, LANES))
        o = dot(p_buf[m], kv_v[...])
        for h in range(4):
            inv = inv_buf[m, h * 64 : (h + 1) * 64, :]
            for t in lane_tiles(LAT):
                part[u, n, h, :, t] = o[h * 64 : (h + 1) * 64, t] * inv

    def pair(u, n):
        theirs = pl.ds(2 * (1 - core), 2)
        return (
            remote(
                lse.at[u, n, theirs], pair_lse.at[u, n],
                pair_send.at[u, n, 0], pair_recv.at[u, n, 0], partner,
            ),
            remote(
                part.at[u, n, theirs], pair_in.at[u, n],
                pair_send.at[u, n, 1], pair_recv.at[u, n, 1], partner,
            ),
        )

    def pair_start(u, n):
        for copy in pair(u, n):
            copy.start()

    def pair_merge(u, n):
        for copy in pair(u, n):
            copy.wait_recv()
        for e in range(2):
            rows = slice(e * 64, (e + 1) * 64)
            mine, theirs = lse[u, n, 2 * core + e], pair_lse[u, n, e]
            top = jnp.maximum(mine, theirs)
            a, b = jnp.exp(mine - top), jnp.exp(theirs - top)
            total = a + b
            inv = 1.0 / total
            a, b = a * inv, b * inv
            for t in lane_tiles(LAT):
                own[u, n, rows, t] = part[u, n, 2 * core + e, :, t] * a + pair_in[u, n, e, :, t] * b
            own_lse[u, n, rows, :] = top + jnp.log(total)

    sides = (at_y(1), at_y(-1))

    def slot_of(hop, e):
        return 0 if hop == 0 else 2 * hop - 1 + e

    def link(side, i, k):
        out, into = ((stat_out, stat_in), (data_out, data_in))[k]
        return remote(
            out.at[side, i], into.at[side, i],
            ring_send.at[side, i, k], ring_recv.at[side, i, k], sides[side],
        )

    def incoming(side, i):
        link(side, i, 0).wait_recv()
        return jnp.broadcast_to(stat_in[side, i, 0:1, :], (LANES, LANES)).T[0:64, :]

    def mix(levels):
        top = functools.reduce(jnp.maximum, levels)
        scales = [jnp.exp(level - top) for level in levels]
        total = functools.reduce(jnp.add, scales)
        inv = 1.0 / total
        return [scale * inv for scale in scales], top + jnp.log(total)

    def send(side, hop, e):
        i, n = slot_of(hop, e), 0 if hop == 0 else side
        rows = slice(e * 64, (e + 1) * 64)
        fresh = hop == 0 or (hop == 1 and e != side)
        level = own_lse[hop, n, rows, :]
        if not fresh:
            j = slot_of(hop - 1, e)
            (a, b), level = mix([level, incoming(side, j)])
        stat_out[side, i] = jnp.concatenate([level, level], axis=0).T[0:8, :]
        link(side, i, 0).start()
        if fresh:
            data_out[side, i] = own[hop, n, rows, :].astype(BF16)
        else:
            link(side, j, 1).wait_recv()
            for t in lane_tiles(LAT):
                mixed = own[hop, n, rows, t] * a + data_in[side, j, :, t].astype(F32) * b
                data_out[side, i, :, t] = mixed.astype(BF16)
        link(side, i, 1).start()

    score(0)
    compute(0)
    pl.semaphore_wait(barrier, len(peers))
    pair_start(0, 0)
    twin = z + 1 - 2 * lax.rem(z, 2)
    w_twin = remote(w_ref, w_v.at[1], twin_send, twin_recv, {"seq": twin})
    w_twin.start()
    by_head(1)
    score(1)
    pair_merge(0, 0)
    send(0, 0, 0)
    send(1, 0, 1)
    compute(1)
    pair_start(1, 0)
    compute(2)
    pair_start(1, 1)
    pair_merge(1, 0)
    send(0, 1, 1)
    compute(3)
    pair_start(2, 0)
    pair_merge(1, 1)
    send(1, 1, 0)
    send(0, 1, 0)
    send(1, 1, 1)
    compute(4)
    pair_start(2, 1)
    pair_merge(2, 0)
    send(0, 2, 1)
    compute(5)
    pair_start(3, 0)
    pair_merge(2, 1)
    send(1, 2, 0)
    send(0, 2, 0)
    send(1, 2, 1)
    compute(6)
    pair_start(3, 1)
    pair_merge(3, 0)
    send(0, 3, 1)
    compute(7)
    pair_start(4, 0)
    pair_merge(3, 1)
    send(1, 3, 0)
    send(0, 3, 0)
    send(1, 3, 1)

    fetch_w.wait()
    fetch_up.wait()
    pad = jnp.zeros((w_v.shape[1], LANES - BLOCK), BF16)

    def w_copy(m, c):
        return remote(w_all.at[m, c], w_all.at[m, c], w_send.at[m], w_recv.at[m], partner)

    for m in range(2):
        if m == 1:
            w_twin.wait_recv()
        for k, t in enumerate(lane_tiles(8 * LANES)):
            columns = w_v[m, :, k * BLOCK : (k + 1) * BLOCK]
            w_all[m, core, :, t] = jnp.concatenate([columns, pad], axis=1)
        w_copy(m, core).start()

    pair_merge(4, 0)
    for e in (1, 0):
        rows, i = slice(e * 64, (e + 1) * 64), slot_of(3, e)
        (a, b, c), _ = mix([own_lse[4, 0, rows, :], incoming(0, i), incoming(1, i)])
        for side in range(2):
            link(side, i, 1).wait_recv()
        merged = jnp.concatenate(
            [
                own[4, 0, rows, t] * a
                + data_in[0, i, :, t].astype(F32) * b
                + data_in[1, i, :, t].astype(F32) * c
                for t in lane_tiles(LAT)
            ],
            axis=1,
        )
        upper = merged.astype(BF16)
        lower = (merged - upper.astype(F32)).astype(BF16)
        value = dot(upper, up_v[e]) + dot(lower, up_v[e])
        val_v[:, e * VDIM : (e + 1) * VDIM] = value.astype(BF16)

    odd = lax.rem(z, 2)
    step = 2 * odd - 1

    def at_target(i):
        return at_z((1, 1, -2, 3)[i] * step, i % 2)

    for i in (3, 2, 1):
        remote(
            val_v, vals.at[i, core], z_send.at[i], z_recv.at[i, core], at_target(i)
        ).start()
    at_pair = remote(val_v, vals.at[0, core], z_send.at[0], z_recv.at[0, core], partner)

    @pl.when(core == 1)
    def _():
        at_pair.start()

    @pl.when(core == 0)
    def _():
        vals[0, 0] = val_v[...]

    def block_of(i):
        return lax.rem(z + step * i + NZ, NZ)

    swap_order = (block_of(core + 2) < block_of(core)).astype(jnp.int32)

    def distance(p):
        return core + 2 * (swap_order if p < 2 else 1 - swap_order)

    def await_half(i, h):
        remote(val_v, vals.at[i, h], z_send.at[0], z_recv.at[i, h], partner).wait_recv()

    for m in range(2):
        w_copy(m, 1 - core).wait_recv()

    def cross(p, k):
        return remote(
            x_out.at[p, k], x_in.at[p, k], x_send.at[p, k], x_recv.at[p, k], at_x(k + 1)
        )

    for p in range(4):
        i, m = distance(p), p % 2
        if m == 0:

            @pl.when(i != 0)
            def _():
                await_half(i, 0)

            await_half(i, 1)
        terms = dot(vals[i, 0], w_all[m, 0]) + dot(vals[i, 1], w_all[m, 1])
        for k, t in enumerate(lane_tiles(8 * LANES)):
            x_f[p, k] = terms[:, t]
        for k in (0, 2, 1):
            to = lax.rem(x + k + 1, NX)
            for c in range(2):
                x_out[p, k, c] = x_f[p, c * NX + to].astype(BF16)
            cross(p, k).start()

    def spread(p, c):
        column = twin if p % 2 else z
        to = {"ctx": y * 2 + c, "seq": block_of(distance(p))}
        return remote(
            z_out.at[p, c], z_in.at[column], a_send.at[p, c], a_recv.at[column], to
        )

    for p in range(4):
        for k in (0, 2, 1):
            cross(p, k).wait_recv()
        for c in range(2):
            total = x_f[p, c * NX + x]
            for k in range(3):
                total = total + x_in[p, k, c].astype(F32)
            z_out[p, c] = total.astype(BF16)
            if c == 0:

                @pl.when(distance(p) == 0)
                def _():
                    z_in[twin if p % 2 else z] = z_out[p, 0]

                @pl.when(distance(p) != 0)
                def _():
                    spread(p, 0).start()

            else:
                spread(p, c).start()

    def last(k):
        to = lax.rem(y + k, NY)
        return remote(z_in.at[to], y_in.at[k], y_send.at[k], y_recv.at[k], at_y(k))

    for block in range(NZ):

        @pl.when(((block != z) & (block != twin)) | (core == 1))
        def _():
            remote(
                z_out.at[0, 0], z_in.at[block], a_send.at[0, 0], a_recv.at[block], partner
            ).wait_recv()

        k = lax.rem(block - y + NY, NY)

        @pl.when(k != 0)
        def _():
            last(k).start()

    total = z_in[y].astype(F32)
    for k in (1, 7, 2, 6, 3, 5, 4):
        last(k).wait_recv()
        total = total + y_in[k].astype(F32)
    out_ref[...] = total[:, :BLOCK].astype(BF16)

    for u in range(5):
        for n in range(1 if u in (0, 4) else 2):
            for copy in pair(u, n):
                copy.wait_send()
    for side in range(2):
        for i in range(7):
            for k in range(2):
                link(side, i, k).wait_send()
    w_twin.wait_send()
    for m in range(2):
        w_copy(m, core).wait_send()
    for i in range(1, 4):
        remote(val_v, vals.at[i, core], z_send.at[i], z_recv.at[i, core], partner).wait_send()

    @pl.when(core == 1)
    def _():
        at_pair.wait_send()

    for p in range(4):
        for k in range(3):
            cross(p, k).wait_send()
        spread(p, 1).wait_send()

        @pl.when(distance(p) != 0)
        def _():
            spread(p, 0).wait_send()

    for k in range(1, NY):
        last(k).wait_send()


def shards(queries, latent_cache, selected, counts, value_up, output_proj_weight):
    rows, heads, width = queries.shape
    tokens = latent_cache.shape[0]
    weight = output_proj_weight[0].reshape(2 * VDIM, output_proj_weight.shape[3])
    hbm = pl.BlockSpec(memory_space=pl.ANY)
    vmem, dma = pltpu.VMEM, pltpu.SemaphoreType.DMA
    return pl.pallas_call(
        kernel,
        out_shape=jax.ShapeDtypeStruct((rows, BLOCK), BF16),
        in_specs=[hbm] * 6,
        out_specs=pl.BlockSpec(memory_space=pltpu.VMEM),
        scratch_shapes=[
            vmem(selected.shape, jnp.int32),
            vmem((1, rows), jnp.int32),
            vmem((2, rows, 16, width), BF16),
            vmem((width, tokens), BF16),
            vmem((2, LAT, VDIM), BF16),
            vmem((2,) + weight.shape, BF16),
            dma((7,)),
            vmem((64, LANES), F32),
            vmem((rows, tokens), F32),
            vmem((tokens, LAT), BF16),
            vmem((heads, rows, width), BF16),
            vmem((2, 256, tokens), F32),
            vmem((2, 256, tokens), BF16),
            vmem((2, 256, LANES), F32),
            vmem((5, 2, 4, rows, LAT), F32),
            vmem((5, 2, 4, rows, LANES), F32),
            vmem((5, 2, 2, rows, LAT), F32),
            vmem((5, 2, 2, rows, LANES), F32),
            dma((5, 2, 2)),
            dma((5, 2, 2)),
            vmem((5, 2, 2 * rows, LAT), F32),
            vmem((5, 2, 2 * rows, LANES), F32),
            vmem((2, 7, rows, LAT), BF16),
            vmem((2, 7, rows, LAT), BF16),
            vmem((2, 7, 8, LANES), F32),
            vmem((2, 7, 8, LANES), F32),
            dma((2, 7, 2)),
            dma((2, 7, 2)),
            vmem((rows, 2 * VDIM), BF16),
            vmem((4, 2, rows, 2 * VDIM), BF16),
            vmem((2, 2, 2 * VDIM, 8 * LANES), BF16),
            dma((2,)),
            dma((2,)),
            dma,
            dma,
            dma((4,)),
            dma((4, 2)),
            vmem((4, 8, rows, LANES), F32),
            vmem((4, 3, 2, rows, LANES), BF16),
            vmem((4, 3, 2, rows, LANES), BF16),
            dma((4, 3)),
            dma((4, 3)),
            vmem((4, 2, rows, LANES), BF16),
            vmem((NZ, rows, LANES), BF16),
            dma((4, 2)),
            dma((NZ,)),
            vmem((NY, rows, LANES), BF16),
            dma((NY,)),
            dma((NY,)),
        ],
        compiler_params=pltpu.CompilerParams(
            collective_id=0, has_side_effects=True, vmem_limit_bytes=60 * 1024 * 1024
        ),
    )(selected, counts.T, queries, latent_cache.T, value_up[0], weight)


def solution(mesh):
    in_specs = (
        P("seq", "head", None),
        P("ctx", None),
        P("seq", "ctx", None),
        P("seq", "ctx"),
        P("head", "ctx", None, None),
        P("head", "ctx", None, "seq"),
    )
    out_specs = P("seq", ("ctx", "head"))
    return jax.shard_map(shards, mesh=mesh, in_specs=in_specs, out_specs=out_specs, check_vma=False)
```

time: 443 us -> 54.1 us (0.12); the launches traced: 438 us -> 54 us
  waiting for transfers between devices: 240 us -> 0 us
  local copies, waits for them, and re-layouts: 116 us -> 1.32 us
  Pallas kernels: 0 us -> 52.6 us
  matrix products: 35.1 us -> 0 us
  blocking collectives: 16.3 us -> 0 us
  between operations: 13.5 us -> 0.01 us
  other arithmetic: 12.2 us -> 0 us
  starting transfers between devices: 5 us -> 0 us
    unnamed x3 -> x0, waiting for transfers between devices: 148 us -> none
    gather x4 -> x0, local copies, waits for them, and re-layouts: 104 us -> none  [attend_group(): collected_latents = latent_cache[rows_blk]]
    all_to_all x1 -> x0, waiting for transfers between devices: 91.8 us -> none  [shards(): lax.all_to_all(part_out[None], 'ctx', split_axis=2, concat_axis=0, tiled=...]
    pallas_call x0 -> x1, Pallas kernels: none -> 52.6 us  [shards(): pl.pallas_call(kernel, out_shape=jax.ShapeDtypeStruct((rows, BLOCK), BF16...]
    dot_general x9 -> x0, matrix products: 29.7 us -> none  [the longest x4 24.4 us: attend_group(): jnp.einsum('epw,etw->ept', query_block_tile, collected_latents, preferred...]
    all_to_all x1 -> x0, blocking collectives: 16.3 us -> none  [shards(): lax.all_to_all(part_lse[None], 'ctx', split_axis=2, concat_axis=0, tiled=...]
    reduce_sum x6 -> x0, other arithmetic: 9.37 us -> none  [the longest x1 8.07 us: fold_sources(): return jnp.sum(factor[..., None] * out_src, axis=0) / norm_sum[..., None]]
    dynamic_update_slice x4 -> x0, local copies, waits for them, and re-layouts: 6.41 us -> none  [shards(): lax.map(partial(attend_group, latent_cache=latent_cache), packed)]
  transfers between devices with their start and end apart: 3 -> 0, of which waited for: 2 -> 0; matrix products, arithmetic and copies ran while one was open for 2% -> 0% of each run, Pallas kernels for 0% -> 0%
where the time goes in v2:
time: 54.1 us; the launch traced here: 54 us
  Pallas kernels  52.6 us (97%)
  local copies, waits for them, and re-layouts  1.32 us (2%)
    pallas_call x1, Pallas kernels, shards(): pl.pallas_call(kernel, out_shape=jax.ShapeDtypeStruct((rows, BLOCK), BF16...  52.6 us
    unnamed x1, local copies, waits for them, and re-layouts  1.32 us

profile of v2, /device:TPU:1, one launch (start us, length us, event | category | flops | bytes accessed | tf_op | source)
XLA Modules:
  0.0 54.0 jit_solution(2742598073636811636)
XLA Ops:
  0.0 52.6 %shard_map.64 = bf16[64,112]{1,0:T(8,128)(2,1)} custom-call(s32[64,1,384]{2,1,0:T(1,128)} %sel_ref.1, s32[1,64]{1,0:T(1,128)} %bitcast.7, bf16[64,32,576]{2,1,0:T(8,128)(2,1)} %q_ref.1, bf16[576,1024]{1,0:T(8,128)(2,1)} %bitcast.4, bf16[2,512,128]{2,1,0:T(8,128)(2,1)} %bitcast.6, bf16[256,896]{1,0:T(8,128)(2,1)} %bitcast.5), custom_call_target="tpu_custom_call" | custom-call | tf_op jit(solution)/shard_map/pallas_call | solution.py:468
  52.6 1.3 %copy.8 = bf16[64,112]{1,0:T(8,128)(2,1)} copy(bf16[64,112]{1,0:T(8,128)(2,1)} %shard_map.64) | data formatting | bytes 28672

commit v3 on v2

--- a/solution.py
+++ b/solution.py
@@ -43,7 +43,7 @@
     return [slice(t * LANES, (t + 1) * LANES) for t in range(width // LANES)]
 
 
-def build_bias(sel_v, cnt_v, words, bias):
+def build_bias(sel_v, cnt_v, words, bias, between):
     tokens = bias.shape[1]
     lane = iota((1, LANES), 1)
     s = sel_v[...].reshape(Q, 384).astype(F32)
@@ -60,6 +60,7 @@
     value = jnp.where(slot < cnt, (1 << (sel_t & 15)).astype(F32), 0.0)
     for k in range(64):
         words[k : k + 1, :] = jnp.sum(jnp.where(high == k, value, 0.0), axis=0, keepdims=True)
+        between(k)
     w = words[...]
     w = (w + pltpu.roll(w, 64, 1)).astype(jnp.int32)
     bytes_t = jnp.concatenate([(w & 255).astype(F32), (w >> 8).astype(F32)], axis=0).T
@@ -75,7 +76,7 @@
     sel_ref, cnt_ref, q_ref, kvt_ref, up_ref, w_ref, out_ref,
     sel_v, cnt_v, q_v, kvt_v, up_v, w_v, local_sem,
     words, bias, kv_v, q_t, s_buf, p_buf, inv_buf,
-    part, lse, pair_in, pair_lse, pair_send, pair_recv, own, own_lse,
+    part, pair_in, pair_send, pair_recv, own, own_lse,
     data_out, data_in, stat_out, stat_in, ring_send, ring_recv,
     val_v, vals, w_all, w_send, w_recv, twin_send, twin_recv, z_send, z_recv,
     x_f, x_out, x_in, x_send, x_recv, z_out, z_in, a_send, a_recv, y_in, y_send, y_recv,
@@ -104,36 +105,57 @@
     fetch_kvt = fetch(2, kvt_ref, kvt_v)
     first_half = lax.rem(y + 4, NY) // 4
     halves = (first_half, 1 - first_half)
-    fetch_q = [
-        fetch(3 + i, q_ref.at[:, pl.ds(pl.multiple_of(half * 16, 16), 16), :], q_v.at[i])
-        for i, half in enumerate(halves)
-    ]
-    fetch_up = fetch(5, up_ref, up_v)
-    fetch_w = fetch(6, w_ref, w_v.at[0])
+
+    def fetch_half(i):
+        heads = pl.ds(pl.multiple_of(halves[i] * 16, 16), 16)
+        return fetch(3 + i, q_ref.at[:, heads, :], q_v.at[i])
+
+    fetch_q = [fetch_half(0)]
 
     barrier = pltpu.get_barrier_semaphore()
     peers = [partner] + [at_y(k) for k in range(1, NY)] + [at_x(k) for k in range(1, NX)]
-    peers += [at_z(k, c) for k in range(1, NZ) for c in range(2)]
+    odd = lax.rem(z, 2)
+    step = 2 * odd - 1
+    twin = z - step
+    ahead = (0, 1, -2, 3)
+    peers += [at_z((core + 2) * step, c) for c in range(2)]
+    peers += [at_z(ahead[i] * step, i % 2) for i in (1, 2, 3)] + [at_z(-step, core)]
+
+    def greet(peer):
+        pl.semaphore_signal(barrier, inc=1, device_id=peer, device_id_type=MESH)
+
     for peer in peers:
-        pl.semaphore_signal(barrier, inc=1, device_id=peer, device_id_type=MESH)
+        greet(peer)
+
+    @pl.when(core == 1)
+    def _():
+        for c in range(2):
+            greet(at_z(step, c))
+
+    entries = len(peers) + 2 * core
 
     fetch_sel.wait()
     fetch_cnt.wait()
-    build_bias(sel_v, cnt_v, words, bias)
-    fetch_kvt.wait()
-    kv_v[...] = kvt_v[0:LAT, :].T
     r, c = iota((256, 256), 0), iota((256, 256), 1)
     swap = (c == (r & 15) * 16 + (r >> 4)).astype(F32).astype(BF16)
 
-    def by_head(i):
-        fetch_q[i].wait()
-        for g in range(Q // 16):
-            block = q_v[i, g * 16 : (g + 1) * 16].reshape(256, width)
-            q_t[pl.ds(halves[i] * 16, 16), g * 16 : (g + 1) * 16, :] = (
-                dot(swap, block).astype(BF16).reshape(16, 16, width)
-            )
-
-    by_head(0)
+    def by_head(i, g):
+        block = q_v[i, g * 16 : (g + 1) * 16].reshape(256, width)
+        q_t[pl.ds(halves[i] * 16, 16), g * 16 : (g + 1) * 16, :] = (
+            dot(swap, block).astype(BF16).reshape(16, 16, width)
+        )
+
+    def between(k):
+        if k == 47:
+            fetch_kvt.wait()
+            fetch_q[0].wait()
+            fetch_q.append(fetch_half(1))
+        if k >= 48 and k % 4 == 0:
+            g = (k - 48) // 4
+            by_head(0, g)
+            kv_v[:, lane_tiles(LAT)[g]] = kvt_v[g * LANES : (g + 1) * LANES, :].T
+
+    build_bias(sel_v, cnt_v, words, bias, between)
 
     def dest(u, n):
         return lax.rem(y + (4 - u if n == 0 else u - 4) + NY, NY)
@@ -147,7 +169,7 @@
     def compute(i):
         if 0 < i < len(sequence) - 1:
             score(i + 1)
-        (u, n), m = sequence[i], i % 2
+        m = i % 2
         for r in range(0, 256, 16):
             h, qs = r // 64, r % 64
             parts = [s_buf[m, r : r + 16, t] + bias[qs : qs + 16, t] for t in lane_tiles(1024)]
@@ -157,44 +179,34 @@
             for t, value in zip(lane_tiles(1024), weights):
                 p_buf[m, r : r + 16, t] = value.astype(BF16)
             level = top * softmax_scale + jnp.log(total)
-            lse[u, n, h, qs : qs + 16, :] = jnp.broadcast_to(level, (16, LANES))
+            part[i, h, qs : qs + 16, LAT:] = jnp.broadcast_to(level, (16, LANES))
             inv_buf[m, r : r + 16, :] = jnp.broadcast_to(1.0 / total, (16, LANES))
         o = dot(p_buf[m], kv_v[...])
         for h in range(4):
             inv = inv_buf[m, h * 64 : (h + 1) * 64, :]
             for t in lane_tiles(LAT):
-                part[u, n, h, :, t] = o[h * 64 : (h + 1) * 64, t] * inv
+                part[i, h, :, t] = o[h * 64 : (h + 1) * 64, t] * inv
 
     def pair(u, n):
-        theirs = pl.ds(2 * (1 - core), 2)
-        return (
-            remote(
-                lse.at[u, n, theirs], pair_lse.at[u, n],
-                pair_send.at[u, n, 0], pair_recv.at[u, n, 0], partner,
-            ),
-            remote(
-                part.at[u, n, theirs], pair_in.at[u, n],
-                pair_send.at[u, n, 1], pair_recv.at[u, n, 1], partner,
-            ),
-        )
+        i, theirs = sequence.index((u, n)), pl.ds(2 * (1 - core), 2)
+        return remote(part.at[i, theirs], pair_in.at[i], pair_send, pair_recv.at[i], partner)
 
     def pair_start(u, n):
-        for copy in pair(u, n):
-            copy.start()
+        pair(u, n).start()
 
     def pair_merge(u, n):
-        for copy in pair(u, n):
-            copy.wait_recv()
+        i = sequence.index((u, n))
+        pair(u, n).wait_recv()
         for e in range(2):
             rows = slice(e * 64, (e + 1) * 64)
-            mine, theirs = lse[u, n, 2 * core + e], pair_lse[u, n, e]
+            mine, theirs = part[i, 2 * core + e, :, LAT:], pair_in[i, e, :, LAT:]
             top = jnp.maximum(mine, theirs)
             a, b = jnp.exp(mine - top), jnp.exp(theirs - top)
             total = a + b
             inv = 1.0 / total
             a, b = a * inv, b * inv
             for t in lane_tiles(LAT):
-                own[u, n, rows, t] = part[u, n, 2 * core + e, :, t] * a + pair_in[u, n, e, :, t] * b
+                own[u, n, rows, t] = part[i, 2 * core + e, :, t] * a + pair_in[i, e, :, t] * b
             own_lse[u, n, rows, :] = top + jnp.log(total)
 
     sides = (at_y(1), at_y(-1))
@@ -206,7 +218,7 @@
         out, into = ((stat_out, stat_in), (data_out, data_in))[k]
         return remote(
             out.at[side, i], into.at[side, i],
-            ring_send.at[side, i, k], ring_recv.at[side, i, k], sides[side],
+            ring_send.at[side, k], ring_recv.at[side, i, k], sides[side],
         )
 
     def incoming(side, i):
@@ -241,12 +253,15 @@
 
     score(0)
     compute(0)
-    pl.semaphore_wait(barrier, len(peers))
+    pl.semaphore_wait(barrier, entries)
     pair_start(0, 0)
-    twin = z + 1 - 2 * lax.rem(z, 2)
     w_twin = remote(w_ref, w_v.at[1], twin_send, twin_recv, {"seq": twin})
     w_twin.start()
-    by_head(1)
+    fetch_q[1].wait()
+    fetch_up = fetch(5, up_ref, up_v)
+    fetch_w = fetch(6, w_ref, w_v.at[0])
+    for g in range(Q // 16):
+        by_head(1, g)
     score(1)
     pair_merge(0, 0)
     send(0, 0, 0)
@@ -319,15 +334,13 @@
         value = dot(upper, up_v[e]) + dot(lower, up_v[e])
         val_v[:, e * VDIM : (e + 1) * VDIM] = value.astype(BF16)
 
-    odd = lax.rem(z, 2)
-    step = 2 * odd - 1
 
     def at_target(i):
-        return at_z((1, 1, -2, 3)[i] * step, i % 2)
+        return at_z(ahead[i] * step, i % 2)
 
     for i in (3, 2, 1):
         remote(
-            val_v, vals.at[i, core], z_send.at[i], z_recv.at[i, core], at_target(i)
+            val_v, vals.at[i, core], z_send.at[1], z_recv.at[i, core], at_target(i)
         ).start()
     at_pair = remote(val_v, vals.at[0, core], z_send.at[0], z_recv.at[0, core], partner)
 
@@ -355,10 +368,13 @@
 
     def cross(p, k):
         return remote(
-            x_out.at[p, k], x_in.at[p, k], x_send.at[p, k], x_recv.at[p, k], at_x(k + 1)
+            x_out.at[p, k], x_in.at[p, k], x_send.at[p], x_recv.at[p], at_x(k + 1)
         )
 
-    for p in range(4):
+    def crossed(p):
+        return remote(x_out.at[p], x_in.at[p], x_send.at[p], x_recv.at[p], partner)
+
+    def produce(p):
         i, m = distance(p), p % 2
         if m == 0:
 
@@ -383,9 +399,8 @@
             z_out.at[p, c], z_in.at[column], a_send.at[p, c], a_recv.at[column], to
         )
 
-    for p in range(4):
-        for k in (0, 2, 1):
-            cross(p, k).wait_recv()
+    def consume(p):
+        crossed(p).wait_recv()
         for c in range(2):
             total = x_f[p, c * NX + x]
             for k in range(3):
@@ -404,9 +419,16 @@
             else:
                 spread(p, c).start()
 
+    for p in range(4):
+        if p >= 2:
+            crossed(p - 2).wait_send()
+        produce(p)
+    for p in range(4):
+        consume(p)
+
     def last(k):
         to = lax.rem(y + k, NY)
-        return remote(z_in.at[to], y_in.at[k], y_send.at[k], y_recv.at[k], at_y(k))
+        return remote(z_in.at[to], y_in.at[k], y_send, y_recv, at_y(k))
 
     for block in range(NZ):
 
@@ -422,41 +444,38 @@
         def _():
             last(k).start()
 
+    others = y_in.at[1:NY]
+    remote(others, others, y_send, y_recv, partner).wait_recv()
     total = z_in[y].astype(F32)
     for k in (1, 7, 2, 6, 3, 5, 4):
-        last(k).wait_recv()
         total = total + y_in[k].astype(F32)
     out_ref[...] = total[:, :BLOCK].astype(BF16)
 
-    for u in range(5):
-        for n in range(1 if u in (0, 4) else 2):
-            for copy in pair(u, n):
-                copy.wait_send()
+    remote(pair_in, pair_in, pair_send, pair_recv.at[0], partner).wait_send()
     for side in range(2):
-        for i in range(7):
-            for k in range(2):
-                link(side, i, k).wait_send()
+        for k, buffer in enumerate((stat_out, data_out)):
+            sent = buffer.at[side]
+            remote(sent, sent, ring_send.at[side, k], ring_recv.at[side, 0, k], partner).wait_send()
     w_twin.wait_send()
     for m in range(2):
         w_copy(m, core).wait_send()
-    for i in range(1, 4):
-        remote(val_v, vals.at[i, core], z_send.at[i], z_recv.at[i, core], partner).wait_send()
+    three = vals.at[1:4, 0]
+    remote(three, three, z_send.at[1], z_recv.at[0, 0], partner).wait_send()
 
     @pl.when(core == 1)
     def _():
         at_pair.wait_send()
 
     for p in range(4):
-        for k in range(3):
-            cross(p, k).wait_send()
+        if p >= 2:
+            crossed(p).wait_send()
         spread(p, 1).wait_send()
 
         @pl.when(distance(p) != 0)
         def _():
             spread(p, 0).wait_send()
 
-    for k in range(1, NY):
-        last(k).wait_send()
+    remote(others, others, y_send, y_recv, partner).wait_send()
 
 
 def shards(queries, latent_cache, selected, counts, value_up, output_proj_weight):
@@ -485,19 +504,17 @@
             vmem((2, 256, tokens), F32),
             vmem((2, 256, tokens), BF16),
             vmem((2, 256, LANES), F32),
-            vmem((5, 2, 4, rows, LAT), F32),
-            vmem((5, 2, 4, rows, LANES), F32),
-            vmem((5, 2, 2, rows, LAT), F32),
-            vmem((5, 2, 2, rows, LANES), F32),
-            dma((5, 2, 2)),
-            dma((5, 2, 2)),
+            vmem((8, 4, rows, LAT + LANES), F32),
+            vmem((8, 2, rows, LAT + LANES), F32),
+            dma,
+            dma((8,)),
             vmem((5, 2, 2 * rows, LAT), F32),
             vmem((5, 2, 2 * rows, LANES), F32),
             vmem((2, 7, rows, LAT), BF16),
             vmem((2, 7, rows, LAT), BF16),
             vmem((2, 7, 8, LANES), F32),
             vmem((2, 7, 8, LANES), F32),
-            dma((2, 7, 2)),
+            dma((2, 2)),
             dma((2, 7, 2)),
             vmem((rows, 2 * VDIM), BF16),
             vmem((4, 2, rows, 2 * VDIM), BF16),
@@ -506,20 +523,20 @@
             dma((2,)),
             dma,
             dma,
-            dma((4,)),
+            dma((2,)),
             dma((4, 2)),
             vmem((4, 8, rows, LANES), F32),
             vmem((4, 3, 2, rows, LANES), BF16),
             vmem((4, 3, 2, rows, LANES), BF16),
-            dma((4, 3)),
-            dma((4, 3)),
+            dma((4,)),
+            dma((4,)),
             vmem((4, 2, rows, LANES), BF16),
             vmem((NZ, rows, LANES), BF16),
             dma((4, 2)),
             dma((NZ,)),
             vmem((NY, rows, LANES), BF16),
-            dma((NY,)),
-            dma((NY,)),
+            dma,
+            dma,
         ],
         compiler_params=pltpu.CompilerParams(
             collective_id=0, has_side_effects=True, vmem_limit_bytes=60 * 1024 * 1024

time: 54.1 us -> 53.2 us (0.983)
  Pallas kernels: 52.6 us -> 51.6 us
    pallas_call x1, Pallas kernels: 52.6 us -> 51.6 us  [shards(): pl.pallas_call(kernel, out_shape=jax.ShapeDtypeStruct((rows, BLOCK), BF16...]
where the time goes in v3:
time: 53.2 us; the launch traced here: 53 us
  Pallas kernels  51.6 us (97%)
  local copies, waits for them, and re-layouts  1.32 us (2%)
    pallas_call x1, Pallas kernels, shards(): pl.pallas_call(kernel, out_shape=jax.ShapeDtypeStruct((rows, BLOCK), BF16...  51.6 us
    unnamed x1, local copies, waits for them, and re-layouts  1.32 us

profile of v3, /device:TPU:1, one launch (start us, length us, event | category | flops | bytes accessed | tf_op | source)
XLA Modules:
  0.0 53.0 jit_solution(4567506206962117173)
XLA Ops:
  0.0 51.6 %shard_map.64 = bf16[64,112]{1,0:T(8,128)(2,1)} custom-call(s32[64,1,384]{2,1,0:T(1,128)} %sel_ref.1, s32[1,64]{1,0:T(1,128)} %bitcast.7, bf16[64,32,576]{2,1,0:T(8,128)(2,1)} %q_ref.1, bf16[576,1024]{1,0:T(8,128)(2,1)} %bitcast.4, bf16[2,512,128]{2,1,0:T(8,128)(2,1)} %bitcast.6, bf16[256,896]{1,0:T(8,128)(2,1)} %bitcast.5), custom_call_target="tpu_custom_call" | custom-call | tf_op jit(solution)/shard_map/pallas_call | solution.py:487
  51.6 1.3 %copy.8 = bf16[64,112]{1,0:T(8,128)(2,1)} copy(bf16[64,112]{1,0:T(8,128)(2,1)} %shard_map.64) | data formatting | bytes 28672

commit v4 on v3

--- a/solution.py
+++ b/solution.py
@@ -240,16 +240,17 @@
         if not fresh:
             j = slot_of(hop - 1, e)
             (a, b), level = mix([level, incoming(side, j)])
+        else:
+            data_out[side, i] = own[hop, n, rows, :].astype(BF16)
+            link(side, i, 1).start()
         stat_out[side, i] = jnp.concatenate([level, level], axis=0).T[0:8, :]
         link(side, i, 0).start()
-        if fresh:
-            data_out[side, i] = own[hop, n, rows, :].astype(BF16)
-        else:
+        if not fresh:
             link(side, j, 1).wait_recv()
             for t in lane_tiles(LAT):
                 mixed = own[hop, n, rows, t] * a + data_in[side, j, :, t].astype(F32) * b
                 data_out[side, i, :, t] = mixed.astype(BF16)
-        link(side, i, 1).start()
+            link(side, i, 1).start()
 
     score(0)
     compute(0)
@@ -304,7 +305,7 @@
     pad = jnp.zeros((w_v.shape[1], LANES - BLOCK), BF16)
 
     def w_copy(m, c):
-        return remote(w_all.at[m, c], w_all.at[m, c], w_send.at[m], w_recv.at[m], partner)
+        return remote(w_all.at[m, c], w_all.at[m, c], w_send, w_recv, partner)
 
     for m in range(2):
         if m == 1:
@@ -340,9 +341,9 @@
 
     for i in (3, 2, 1):
         remote(
-            val_v, vals.at[i, core], z_send.at[1], z_recv.at[i, core], at_target(i)
+            val_v, vals.at[i, core], z_send.at[1], z_recv.at[i], at_target(i)
         ).start()
-    at_pair = remote(val_v, vals.at[0, core], z_send.at[0], z_recv.at[0, core], partner)
+    at_pair = remote(val_v, vals.at[0, core], z_send.at[0], z_recv.at[0], partner)
 
     @pl.when(core == 1)
     def _():
@@ -360,11 +361,11 @@
     def distance(p):
         return core + 2 * (swap_order if p < 2 else 1 - swap_order)
 
-    def await_half(i, h):
-        remote(val_v, vals.at[i, h], z_send.at[0], z_recv.at[i, h], partner).wait_recv()
-
-    for m in range(2):
-        w_copy(m, 1 - core).wait_recv()
+    def await_values(i, into):
+        remote(into, into, z_send.at[0], z_recv.at[i], partner).wait_recv()
+
+    both = w_all.at[0]
+    remote(both, both, w_send, w_recv, partner).wait_recv()
 
     def cross(p, k):
         return remote(
@@ -380,9 +381,12 @@
 
             @pl.when(i != 0)
             def _():
-                await_half(i, 0)
-
-            await_half(i, 1)
+                await_values(i, vals.at[i])
+
+            @pl.when(i == 0)
+            def _():
+                await_values(0, vals.at[0, 1])
+
         terms = dot(vals[i, 0], w_all[m, 0]) + dot(vals[i, 1], w_all[m, 1])
         for k, t in enumerate(lane_tiles(8 * LANES)):
             x_f[p, k] = terms[:, t]
@@ -396,7 +400,7 @@
         column = twin if p % 2 else z
         to = {"ctx": y * 2 + c, "seq": block_of(distance(p))}
         return remote(
-            z_out.at[p, c], z_in.at[column], a_send.at[p, c], a_recv.at[column], to
+            z_out.at[p, c], z_in.at[column], a_send.at[4 if c else p], a_recv.at[column], to
         )
 
     def consume(p):
@@ -435,7 +439,7 @@
         @pl.when(((block != z) & (block != twin)) | (core == 1))
         def _():
             remote(
-                z_out.at[0, 0], z_in.at[block], a_send.at[0, 0], a_recv.at[block], partner
+                z_out.at[0, 0], z_in.at[block], a_send.at[0], a_recv.at[block], partner
             ).wait_recv()
 
         k = lax.rem(block - y + NY, NY)
@@ -457,10 +461,9 @@
             sent = buffer.at[side]
             remote(sent, sent, ring_send.at[side, k], ring_recv.at[side, 0, k], partner).wait_send()
     w_twin.wait_send()
-    for m in range(2):
-        w_copy(m, core).wait_send()
+    remote(both, both, w_send, w_recv, partner).wait_send()
     three = vals.at[1:4, 0]
-    remote(three, three, z_send.at[1], z_recv.at[0, 0], partner).wait_send()
+    remote(three, three, z_send.at[1], z_recv.at[0], partner).wait_send()
 
     @pl.when(core == 1)
     def _():
@@ -469,13 +472,13 @@
     for p in range(4):
         if p >= 2:
             crossed(p).wait_send()
-        spread(p, 1).wait_send()
-
         @pl.when(distance(p) != 0)
         def _():
             spread(p, 0).wait_send()
 
     remote(others, others, y_send, y_recv, partner).wait_send()
+    second = z_out.at[:, 1]
+    remote(second, second, a_send.at[4], a_recv.at[0], partner).wait_send()
 
 
 def shards(queries, latent_cache, selected, counts, value_up, output_proj_weight):
@@ -519,12 +522,12 @@
             vmem((rows, 2 * VDIM), BF16),
             vmem((4, 2, rows, 2 * VDIM), BF16),
             vmem((2, 2, 2 * VDIM, 8 * LANES), BF16),
+            dma,
+            dma,
+            dma,
+            dma,
             dma((2,)),
-            dma((2,)),
-            dma,
-            dma,
-            dma((2,)),
-            dma((4, 2)),
+            dma((4,)),
             vmem((4, 8, rows, LANES), F32),
             vmem((4, 3, 2, rows, LANES), BF16),
             vmem((4, 3, 2, rows, LANES), BF16),
@@ -532,7 +535,7 @@
             dma((4,)),
             vmem((4, 2, rows, LANES), BF16),
             vmem((NZ, rows, LANES), BF16),
-            dma((4, 2)),
+            dma((5,)),
             dma((NZ,)),
             vmem((NY, rows, LANES), BF16),
             dma,

time: 53.2 us -> 53.5 us (level)
  no operation moved by 1% of the time
where the time goes in v4:
time: 53.5 us; the launch traced here: 53.3 us
  Pallas kernels  52 us (97%)
  local copies, waits for them, and re-layouts  1.32 us (2%)
    pallas_call x1, Pallas kernels, shards(): pl.pallas_call(kernel, out_shape=jax.ShapeDtypeStruct((rows, BLOCK), BF16...  52 us
    unnamed x1, local copies, waits for them, and re-layouts  1.32 us

profile of v4, /device:TPU:1, one launch (start us, length us, event | category | flops | bytes accessed | tf_op | source)
XLA Modules:
  0.0 53.3 jit_solution(3292819985934691757)
XLA Ops:
  0.0 52.0 %shard_map.64 = bf16[64,112]{1,0:T(8,128)(2,1)} custom-call(s32[64,1,384]{2,1,0:T(1,128)} %sel_ref.1, s32[1,64]{1,0:T(1,128)} %bitcast.7, bf16[64,32,576]{2,1,0:T(8,128)(2,1)} %q_ref.1, bf16[576,1024]{1,0:T(8,128)(2,1)} %bitcast.4, bf16[2,512,128]{2,1,0:T(8,128)(2,1)} %bitcast.6, bf16[256,896]{1,0:T(8,128)(2,1)} %bitcast.5), custom_call_target="tpu_custom_call" | custom-call | tf_op jit(solution)/shard_map/pallas_call | solution.py:490
  52.0 1.3 %copy.8 = bf16[64,112]{1,0:T(8,128)(2,1)} copy(bf16[64,112]{1,0:T(8,128)(2,1)} %shard_map.64) | data formatting | bytes 28672

commit v5 on v3

--- a/solution.py
+++ b/solution.py
@@ -422,8 +422,10 @@
     for p in range(4):
         if p >= 2:
             crossed(p - 2).wait_send()
+        if p == 3:
+            consume(0)
         produce(p)
-    for p in range(4):
+    for p in range(1, 4):
         consume(p)
 
     def last(k):

time: 53.2 us -> 53.2 us (level)
  no operation moved by 1% of the time
where the time goes in v5:
time: 53.2 us; the launch traced here: 52.8 us
  Pallas kernels  51.5 us (97%)
  local copies, waits for them, and re-layouts  1.32 us (2%)
    pallas_call x1, Pallas kernels, shards(): pl.pallas_call(kernel, out_shape=jax.ShapeDtypeStruct((rows, BLOCK), BF16...  51.5 us
    unnamed x1, local copies, waits for them, and re-layouts  1.32 us

profile of v5, /device:TPU:1, one launch (start us, length us, event | category | flops | bytes accessed | tf_op | source)
XLA Modules:
  0.0 52.8 jit_solution(9969509469797658071)
XLA Ops:
  0.0 51.5 %shard_map.64 = bf16[64,112]{1,0:T(8,128)(2,1)} custom-call(s32[64,1,384]{2,1,0:T(1,128)} %sel_ref.1, s32[1,64]{1,0:T(1,128)} %bitcast.7, bf16[64,32,576]{2,1,0:T(8,128)(2,1)} %q_ref.1, bf16[576,1024]{1,0:T(8,128)(2,1)} %bitcast.4, bf16[2,512,128]{2,1,0:T(8,128)(2,1)} %bitcast.6, bf16[256,896]{1,0:T(8,128)(2,1)} %bitcast.5), custom_call_target="tpu_custom_call" | custom-call | tf_op jit(solution)/shard_map/pallas_call | solution.py:489
  51.5 1.3 %copy.8 = bf16[64,112]{1,0:T(8,128)(2,1)} copy(bf16[64,112]{1,0:T(8,128)(2,1)} %shard_map.64) | data formatting | bytes 28672
